TPU v7x, 256 devices: a whole 4x4x8 slice. The times are simulated.
256 devices in a mesh: gz: 16 (over y_lo, z), gy: 16 (over y_hi, x, core).
Axes of the slice: x: 4, y: 4 (y_hi: 2, y_lo: 2; y = y_hi * 2 + y_lo), z: 8, core: 2. Of those that a mesh axis runs over, the one named last changes fastest.
Arguments:
- velocity: float32 [2, 6, 4096, 4096], P(None, None, 'gy', 'gz'), may hold values from -6 to 6
Outputs:
- spectrum: float32 [2, 6, 4096, 4096], P(None, None, 'gy', 'gz')
All inputs are finite; a program needn't handle non-finite values.
Results may differ from a plain program's by a relative error of at most 0.000098.
Values sent between devices are 32-bit elements; how exact they have to be, the bound alone decides.
A program may use at most 64 MiB of HBM per device.

v0:
```python
import math

import jax
import jax.numpy as jnp
from jax import lax
from jax.sharding import PartitionSpec as P


def swapped(block, axis, distance):
    count = lax.axis_size(axis)
    route = []
    for low in range(count):
        high = low | 1 << distance
        if high != low and high < count:
            route += [(low, high), (high, low)]
    return lax.ppermute(block, axis, route)


def reversed_index(my_index, bit_count):
    result = my_index * 0
    for place in range(bit_count):
        result = result + my_index // 2**place % 2 * 2 ** (bit_count - 1 - place)
    return result


def phases(products, length):
    return -2.0 * math.pi * (products % length).astype(jnp.float32) / length


def twist(values, cosine, sine):
    real_part = values[0]
    imag_part = values[1]
    return jnp.stack([real_part * cosine - imag_part * sine, real_part * sine + imag_part * cosine])


def complex_product(form, values, cosine, sine):

    def single(left, right):
        return jnp.einsum(form, left, right, precision=lax.Precision.HIGHEST)

    real_part = values[0]
    imag_part = values[1]
    return jnp.stack(
        [
            single(real_part, cosine) - single(imag_part, sine),
            single(real_part, sine) + single(imag_part, cosine),
        ]
    )


def dft_tables(length, factor):
    positions = jnp.arange(length, dtype=jnp.int32)
    phase = phases(positions[:, None] * positions[None, :], length)
    return (jnp.cos(phase) * factor, jnp.sin(phase) * factor)


def butterfly(own_block, partner_block, my_index, bit):
    upper_bit = my_index // 2**bit % 2
    lower_bits = my_index % 2**bit
    period = 2 ** (bit + 1)
    flip = (1 - 2 * upper_bit).astype(jnp.float32)
    mixed = own_block * flip + partner_block
    phase = phases(lower_bits * upper_bit, period)
    return twist(mixed, jnp.cos(phase), jnp.sin(phase))


def finish_last(values, frequency, length):
    local_len = values.shape[3]
    positions = jnp.arange(local_len, dtype=jnp.int32)
    phase = phases(positions * frequency, length)
    twisted = twist(values, jnp.cos(phase), jnp.sin(phase))
    cosine, sine = dft_tables(local_len, 1.0 / math.sqrt(length))
    return complex_product("ayl,lk->ayk", twisted, cosine, sine)


def finish_middle(values, frequency, length):
    local_len = values.shape[2]
    positions = jnp.arange(local_len, dtype=jnp.int32)
    phase = phases(positions * frequency, length)[:, None]
    twisted = twist(values, jnp.cos(phase), jnp.sin(phase))
    cosine, sine = dft_tables(local_len, 1.0 / math.sqrt(length))
    return complex_product("alz,lk->akz", twisted, cosine, sine)


def shards(velocity):
    z_count = lax.axis_size("gz")
    y_count = lax.axis_size("gy")
    z_bits = z_count.bit_length() - 1
    y_bits = y_count.bit_length() - 1
    local_y = velocity.shape[2]
    local_z = velocity.shape[3]
    z_index = lax.axis_index("gz")
    y_index = lax.axis_index("gy")
    z_length = z_count * local_z
    y_length = y_count * local_y
    current = velocity
    for section in range(z_bits):
        bit = z_bits - 1 - section
        partner_block = swapped(current, "gz", bit)
        current = butterfly(current, partner_block, z_index, bit)
    current = finish_last(current, reversed_index(z_index, z_bits), z_length)
    for section in range(y_bits):
        bit = y_bits - 1 - section
        partner_block = swapped(current, "gy", bit)
        current = butterfly(current, partner_block, y_index, bit)
    result = finish_middle(current, reversed_index(y_index, y_bits), y_length)
    return result


def solution(mesh):
    in_specs = (P(None, None, "gy", "gz"),)
    out_specs = P(None, None, "gy", "gz")
    return jax.shard_map(shards, mesh=mesh, in_specs=in_specs, out_specs=out_specs, check_vma=False)
```

profile of v0, /device:TPU:8, one launch (start us, length us, event | category | flops | bytes accessed | tf_op | source)
XLA Modules:
  0.0 692.1 jit_solution(4309956665386972427)
XLA Ops:
  0.0 2.2 collective-permute-start
  2.3 67.7 %collective-permute-done = f32[2,6,256,256]{3,2,1,0:T(8,128)S(1)} collective-permute-done((f32[2,6,256,256]{3,2,1,0:T(8,128)}, f32[2,6,256,256]{3,2,1,0:T(8,128)S(1)}, u32[]{:S(2)}, u32[]{:S(2)}) %collective-permute-start) | collective-permute-done | bytes 3145760 | tf_op jit(solution)/shard_map/ppermute | solution.py:16
  70.1 2.3 multiply_add_fusion.7
  72.4 0.5 multiply_subtract_fusion.9
  72.8 2.1 pad_maximum_fusion
  74.9 7.2 %collective-permute-start.1 = (f32[2,6,256,256]{3,2,1,0:T(8,128)}, f32[2,6,256,256]{3,2,1,0:T(8,128)}, u32[]{:S(2)}, u32[]{:S(2)}) collective-permute-start(f32[2,6,256,256]{3,2,1,0:T(8,128)} %pad_maximum_fusion), channel_id=1, source_target_pairs={{0,64},{64,0},{16,80},{80,16},{32,96},{96,32},{48,112},{112,48},{1... | collective-permute-start | bytes 9437192 | tf_op jit(solution)/shard_map/ppermute | solution.py:16
  82.2 134.3 %collective-permute-done.1 = f32[2,6,256,256]{3,2,1,0:T(8,128)} collective-permute-done((f32[2,6,256,256]{3,2,1,0:T(8,128)}, f32[2,6,256,256]{3,2,1,0:T(8,128)}, u32[]{:S(2)}, u32[]{:S(2)}) %collective-permute-start.1) | collective-permute-done | bytes 3145760 | tf_op jit(solution)/shard_map/ppermute | solution.py:16
  216.5 2.3 multiply_add_fusion.6
  218.8 0.5 multiply_subtract_fusion.8
  219.3 2.1 pad_maximum_fusion.1
  221.3 2.6 collective-permute-start.2
  224.1 135.0 %collective-permute-done.2 = f32[2,6,256,256]{3,2,1,0:T(8,128)} collective-permute-done((f32[2,6,256,256]{3,2,1,0:T(8,128)}, f32[2,6,256,256]{3,2,1,0:T(8,128)}, u32[]{:S(2)}, u32[]{:S(2)}) %collective-permute-start.2) | collective-permute-done | bytes 3145760 | tf_op jit(solution)/shard_map/ppermute | solution.py:16
  359.1 2.3 multiply_add_fusion.5
  361.4 0.5 multiply_subtract_fusion.7
  361.9 2.1 pad_maximum_fusion.2
  363.9 0.0 collective-permute-start.3
  363.9 0.1 fusion.42
  364.0 70.0 %collective-permute-done.3 = f32[2,6,256,256]{3,2,1,0:T(8,128)} collective-permute-done((f32[2,6,256,256]{3,2,1,0:T(8,128)}, f32[2,6,256,256]{3,2,1,0:T(8,128)}, u32[]{:S(2)}, u32[]{:S(2)}) %collective-permute-start.3) | collective-permute-done | bytes 3145760 | tf_op jit(solution)/shard_map/ppermute | solution.py:16
  433.9 2.3 multiply_add_fusion.4
  436.2 0.3 multiply_subtract_fusion.6
  436.6 2.5 fusion.1
  439.0 2.4 fusion
  441.5 2.5 subtract_bitcast_fusion.1
  444.0 2.4 add_bitcast_fusion.1
  446.4 2.1 pad_maximum_fusion.3
  448.5 2.3 collective-permute-start.4
  450.9 68.2 %collective-permute-done.4 = f32[2,6,256,256]{3,2,1,0:T(8,128)} collective-permute-done((f32[2,6,256,256]{3,2,1,0:T(8,128)}, f32[2,6,256,256]{3,2,1,0:T(8,128)}, u32[]{:S(2)}, u32[]{:S(2)}) %collective-permute-start.4) | collective-permute-done | bytes 3145760 | tf_op jit(solution)/shard_map/ppermute | solution.py:16
  519.1 2.3 multiply_add_fusion.3
  521.4 0.5 multiply_subtract_fusion.4
  521.9 2.1 pad_maximum_fusion.4
  523.9 3.0 collective-permute-start.5
  527.1 66.5 %collective-permute-done.5 = f32[2,6,256,256]{3,2,1,0:T(8,128)} collective-permute-done((f32[2,6,256,256]{3,2,1,0:T(8,128)}, f32[2,6,256,256]{3,2,1,0:T(8,128)}, u32[]{:S(2)}, u32[]{:S(2)}) %collective-permute-start.5) | collective-permute-done | bytes 3145760 | tf_op jit(solution)/shard_map/ppermute | solution.py:16
  593.6 2.3 multiply_add_fusion.2
  595.9 0.5 multiply_subtract_fusion.3
  596.4 2.1 pad_maximum_fusion.5
  598.5 1.5 collective-permute-start.6
  600.1 65.6 %collective-permute-done.6 = f32[2,6,256,256]{3,2,1,0:T(8,128)} collective-permute-done((f32[2,6,256,256]{3,2,1,0:T(8,128)}, f32[2,6,256,256]{3,2,1,0:T(8,128)}, u32[]{:S(2)}, u32[]{:S(2)}) %collective-permute-start.6) | collective-permute-done | bytes 3145760 | tf_op jit(solution)/shard_map/ppermute | solution.py:16
  665.8 2.3 multiply_add_fusion.1
  668.1 0.5 multiply_subtract_fusion.2
  668.5 2.1 pad_maximum_fusion.6
  670.6 0.0 collective-permute-start.7
  670.6 0.1 fusion.40
  670.6 5.9 collective-permute-done.7
  676.6 2.3 multiply_add_fusion
  678.9 2.8 fusion.6
  681.7 2.8 fusion.12
  684.5 2.8 subtract_bitcast_fusion
  687.3 2.8 add_bitcast_fusion
  690.1 2.1 pad_maximum_fusion.7
Async XLA Ops:
  0.0 70.1 %collective-permute-start = (f32[2,6,256,256]{3,2,1,0:T(8,128)}, f32[2,6,256,256]{3,2,1,0:T(8,128)S(1)}, u32[]{:S(2)}, u32[]{:S(2)}) collective-permute-start(f32[2,6,256,256]{3,2,1,0:T(8,128)} %param.1), channel_id=1, source_target_pairs={{0,128},{128,0},{16,144},{144,16},{32,160},{160,32},{48,176},{176,... | collective-permute-start | bytes 9437192 | tf_op jit(solution)/shard_map/ppermute | solution.py:16
  74.9 141.6 %collective-permute-start.1 = (f32[2,6,256,256]{3,2,1,0:T(8,128)}, f32[2,6,256,256]{3,2,1,0:T(8,128)}, u32[]{:S(2)}, u32[]{:S(2)}) collective-permute-start(f32[2,6,256,256]{3,2,1,0:T(8,128)} %pad_maximum_fusion), channel_id=1, source_target_pairs={{0,64},{64,0},{16,80},{80,16},{32,96},{96,32},{48,112},{112,48},{1... | collective-permute-start | bytes 9437192 | tf_op jit(solution)/shard_map/ppermute | solution.py:16
  221.3 137.8 %collective-permute-start.2 = (f32[2,6,256,256]{3,2,1,0:T(8,128)}, f32[2,6,256,256]{3,2,1,0:T(8,128)}, u32[]{:S(2)}, u32[]{:S(2)}) collective-permute-start(f32[2,6,256,256]{3,2,1,0:T(8,128)} %pad_maximum_fusion.1), channel_id=1, source_target_pairs={{0,32},{32,0},{16,48},{48,16},{64,96},{96,64},{80,112},{112,80},{1... | collective-permute-start | bytes 9437192 | tf_op jit(solution)/shard_map/ppermute | solution.py:16
  363.9 70.0 %collective-permute-start.3 = (f32[2,6,256,256]{3,2,1,0:T(8,128)}, f32[2,6,256,256]{3,2,1,0:T(8,128)}, u32[]{:S(2)}, u32[]{:S(2)}) collective-permute-start(f32[2,6,256,256]{3,2,1,0:T(8,128)} %pad_maximum_fusion.2), channel_id=1, source_target_pairs={{0,16},{16,0},{32,48},{48,32},{64,80},{80,64},{96,112},{112,96},{1... | collective-permute-start | bytes 9437192 | tf_op jit(solution)/shard_map/ppermute | solution.py:16
  448.5 70.6 %collective-permute-start.4 = (f32[2,6,256,256]{3,2,1,0:T(8,128)}, f32[2,6,256,256]{3,2,1,0:T(8,128)}, u32[]{:S(2)}, u32[]{:S(2)}) collective-permute-start(f32[2,6,256,256]{3,2,1,0:T(8,128)} %pad_maximum_fusion.3), channel_id=1, source_target_pairs={{0,8},{8,0},{1,9},{9,1},{2,10},{10,2},{3,11},{11,3},{4,12},{12,4},... | collective-permute-start | bytes 9437192 | tf_op jit(solution)/shard_map/ppermute | solution.py:16
  523.9 69.7 %collective-permute-start.5 = (f32[2,6,256,256]{3,2,1,0:T(8,128)}, f32[2,6,256,256]{3,2,1,0:T(8,128)}, u32[]{:S(2)}, u32[]{:S(2)}) collective-permute-start(f32[2,6,256,256]{3,2,1,0:T(8,128)} %pad_maximum_fusion.4), channel_id=1, source_target_pairs={{0,4},{4,0},{1,5},{5,1},{2,6},{6,2},{3,7},{7,3},{8,12},{12,8},{9,1... | collective-permute-start | bytes 9437192 | tf_op jit(solution)/shard_map/ppermute | solution.py:16
  598.5 67.3 %collective-permute-start.6 = (f32[2,6,256,256]{3,2,1,0:T(8,128)}, f32[2,6,256,256]{3,2,1,0:T(8,128)}, u32[]{:S(2)}, u32[]{:S(2)}) collective-permute-start(f32[2,6,256,256]{3,2,1,0:T(8,128)} %pad_maximum_fusion.5), channel_id=1, source_target_pairs={{0,2},{2,0},{1,3},{3,1},{4,6},{6,4},{5,7},{7,5},{8,10},{10,8},{9,1... | collective-permute-start | bytes 9437192 | tf_op jit(solution)/shard_map/ppermute | solution.py:16
  670.6 6.0 collective-permute-start.7
where the time goes:
time: 694 us; the launch traced here: 692 us
  waiting for transfers between devices  613 us (88%)
  other arithmetic  38 us (5%)
  matrix products  21 us (3%)
  starting transfers between devices  18.8 us (3%)
    ppermute x8, waiting for transfers between devices, swapped(): return lax.ppermute(block, axis, route)  613 us
    dot_general x8, matrix products, single(): return jnp.einsum(form, left, right, precision=lax.Precision.HIGHEST)  21 us
    ppermute x8, starting transfers between devices, swapped(): return lax.ppermute(block, axis, route)  18.8 us
    add x8, other arithmetic, butterfly(): mixed = own_block * flip + partner_block  18.4 us
  transfers between devices with their start and end apart: 8, of which 8 were waited for; matrix products, arithmetic and copies ran while one was open for 0% of the time, Pallas kernels for 0%

commit v1 on v0

v1 whole, which is shorter than its diff:
```python
import functools

import jax
import jax.numpy as jnp
import ml_dtypes
import numpy as np
from jax import lax
from jax.experimental import pallas as pl
from jax.experimental.pallas import tpu as pltpu
from jax.sharding import PartitionSpec as P

MESH = pl.DeviceIdType.MESH
F32 = jnp.float32
BF16 = jnp.bfloat16
CHUNKS = 3
NZD = 8
NQD = 32


def reversed_bits(value):
    return int(format(value, "04b")[::-1], 2)


def split_host(table):
    high = table.astype(np.float32).astype(ml_dtypes.bfloat16)
    low = (table - high.astype(np.float64)).astype(ml_dtypes.bfloat16)
    return np.stack([high, low])


def device_table():
    index = np.arange(256)
    q, z = index // NZD, index % NZD
    cz, cy = q // 16 * 8 + z, q % 16
    kz = np.array([reversed_bits(c) for c in cz])
    ky = np.array([reversed_bits(c) for c in cy])
    phase = -2.0 * np.pi * ((kz[:, None] * cz[None, :] + ky[:, None] * cy[None, :]) % 16) / 16
    c, s = np.cos(phase), np.sin(phase)
    return split_host(np.block([[c, -s], [s, c]]))


def local_table():
    index = np.arange(256)
    phase = -2.0 * np.pi * ((index[:, None] * index[None, :]) % 256) / 256
    return (np.stack([np.cos(phase), np.sin(phase)]) / 64).astype(np.float32)


def twiddle_table():
    frequency = np.array([reversed_bits(c) for c in range(16)])
    phase = -2.0 * np.pi * ((frequency[:, None] * np.arange(256)[None, :]) % 4096) / 4096
    both = np.stack([np.cos(phase), np.sin(phase)], axis=1).astype(np.float32)
    return np.repeat(both[:, :, None, :], 8, axis=2)


def split(values):
    high = values.astype(BF16)
    return high, (values - high.astype(F32)).astype(BF16)


def mm(left, right):
    return jnp.dot(left, right, preferred_element_type=F32)


def kernel(
    x_hbm, gdev_hbm, floc_hbm, twid_hbm, o_hbm,
    xin, send_p, recv_p, mid_in, mid_out, recv_q, recv_r, out, gdev, floc, twid, ytab, ztab,
    in_sem, const_sem, out_sem, psend, precv, qsend, qrecv, bsend, brecv, rsend, rrecv,
):
    gz, gy = lax.axis_index("gz"), lax.axis_index("gy")
    yl, z = gz // 8, gz % 8
    yh, xc, co = gy // 8, gy // 2 % 4, gy % 2
    yc = yh * 2 + yl
    q = yl * 16 + gy

    def z_partner(t):
        zt = (z + t) % 8
        return zt, (yl * 8 + zt, gy)

    def q_partner(t):
        y2, x2, c2 = (yc + t // 8) % 4, (xc + t // 2 % 4) % 4, (co + t % 2) % 2
        gy2 = y2 // 2 * 8 + x2 * 2 + c2
        return y2 % 2 * 16 + gy2, (y2 % 2 * 8 + z, gy2)

    loads = [pltpu.make_async_copy(x_hbm.at[:, pl.ds(2 * c, 2)], xin.at[:, pl.ds(2 * c, 2)], in_sem.at[c]) for c in range(CHUNKS)]
    for copy in loads:
        copy.start()
    consts = [
        pltpu.make_async_copy(floc_hbm, floc, const_sem.at[0]),
        pltpu.make_async_copy(twid_hbm, twid, const_sem.at[1]),
        pltpu.make_async_copy(gdev_hbm, gdev, const_sem.at[2]),
    ]
    for copy in consts:
        copy.start()

    barrier = pltpu.get_barrier_semaphore()

    @pl.loop(1, 8)
    def _(t):
        pl.semaphore_signal(barrier, inc=1, device_id=z_partner(t)[1], device_id_type=MESH)

    @pl.loop(1, 32)
    def _(t):
        pl.semaphore_signal(barrier, inc=1, device_id=q_partner(t)[1], device_id_type=MESH)

    def relayout(c):
        flat = send_p.at[c].reshape(2048, 128)
        for p in range(2):
            for r in range(2):
                for h in range(2):
                    flat[pl.ds(p * 4 + r * 2 + h, 256, stride=8), :] = xin[r, 2 * c + p, :, h * 128 : h * 128 + 128]

    def p_copy(c, t):
        zt, target = z_partner(t)
        return pltpu.make_async_remote_copy(
            send_p.at[c, pl.ds(zt * 32, 32)], recv_p.at[c, z], psend.at[c, t], precv.at[c, t], device_id=target, device_id_type=MESH
        )

    def p_own(c):
        return pltpu.make_async_copy(send_p.at[c, pl.ds(z * 32, 32)], recv_p.at[c, z], precv.at[c, 0])

    def q_copy(c, t):
        qt, target = q_partner(t)
        return pltpu.make_async_remote_copy(
            recv_p.at[c, :, qt], mid_in.at[c, pl.ds(q * 8, 8)], qsend.at[c, t], qrecv.at[c, t], device_id=target, device_id_type=MESH
        )

    def q_own(c):
        return pltpu.make_async_copy(recv_p.at[c, :, q], mid_in.at[c, pl.ds(q * 8, 8)], qrecv.at[c, 0])

    def b_copy(c, t):
        qt, target = q_partner(t)
        return pltpu.make_async_remote_copy(
            mid_out.at[c, pl.ds(qt * 8, 8)], recv_q.at[c, :, q], bsend.at[c, t], brecv.at[c, t], device_id=target, device_id_type=MESH
        )

    def b_own(c):
        return pltpu.make_async_copy(mid_out.at[c, pl.ds(q * 8, 8)], recv_q.at[c, :, q], brecv.at[c, 0])

    def r_copy(c, t):
        zt, target = z_partner(t)
        return pltpu.make_async_remote_copy(
            recv_q.at[c, zt], recv_r.at[c, pl.ds(z * 32, 32)], rsend.at[c, t], rrecv.at[c, t], device_id=target, device_id_type=MESH
        )

    def r_own(c):
        return pltpu.make_async_copy(recv_q.at[c, z], recv_r.at[c, pl.ds(z * 32, 32)], rrecv.at[c, 0])

    def start(copy, own, count, c):
        own(c).start()

        @pl.loop(1, count)
        def _(t):
            copy(c, t).start()

    def arrived(copy, own, count, c):
        own(c).wait()

        @pl.loop(1, count)
        def _(t):
            copy(c, t).wait_recv()

    def arrived_some(copy, c, low, high):
        @pl.loop(low, high)
        def _(t):
            copy(c, t).wait_recv()

    def sent(copy, count):
        for c in range(CHUNKS):

            @pl.loop(1, count)
            def _(t):
                copy(c, t).wait_send()

    def read_rows(ref):
        flat = ref.reshape(2048, 128)
        rows = [
            jnp.concatenate([flat[pl.ds(p * 4 + r * 2 + h, 256, stride=8), :] for p in range(2) for h in range(2)], axis=1)
            for r in range(2)
        ]
        return jnp.concatenate(rows, axis=0)

    def middle(c):
        xh, xl = split(read_rows(mid_in.at[c]))
        y = mm(gdev[0], xh) + mm(gdev[0], xl) + mm(gdev[1], xh)
        flat = mid_out.at[c].reshape(2048, 128)
        for p in range(2):
            for r in range(2):
                for h in range(2):
                    flat[pl.ds(p * 4 + r * 2 + h, 256, stride=8), :] = y[r * 256 : r * 256 + 256, (p * 2 + h) * 128 : (p * 2 + h) * 128 + 128]

    def tables():
        fr, fi = floc[0], floc[1]

        def twisted(position):
            tc, ts = twid[position, 0, 0:1], twid[position, 1, 0:1]
            return fr * tc - fi * ts, fr * ts + fi * tc

        a, b = twisted(gy)
        full = jnp.concatenate([jnp.concatenate([a, -b], axis=1), jnp.concatenate([b, a], axis=1)], axis=0)
        high, low = split(full)
        ytab[0] = high
        ytab[1] = low
        a, b = twisted(gz)
        a, b = a.T, b.T
        full = jnp.concatenate([jnp.concatenate([a, b], axis=1), jnp.concatenate([-b, a], axis=1)], axis=0)
        high, low = split(full)
        ztab[0] = high
        ztab[1] = low

    def store(c):
        return pltpu.make_async_copy(out.at[:, pl.ds(2 * c, 2)], o_hbm.at[:, pl.ds(2 * c, 2)], out_sem.at[c])

    def final(c):
        xh, xl = split(read_rows(recv_r.at[c]))
        u = mm(ytab[0], xh) + mm(ytab[0], xl) + mm(ytab[1], xh)
        for p in range(2):
            w = jnp.concatenate([u[:256, p * 256 : p * 256 + 256], u[256:, p * 256 : p * 256 + 256]], axis=1)
            wh, wl = split(w)
            v = mm(wh, ztab[0]) + mm(wl, ztab[0]) + mm(wh, ztab[1])
            out[0, 2 * c + p] = v[:, :256]
            out[1, 2 * c + p] = v[:, 256:]
        store(c).start()

    PZ = functools.partial
    loads[0].wait()
    relayout(0)
    pl.semaphore_wait(barrier, 38)
    start(p_copy, p_own, 8, 0)
    loads[1].wait()
    relayout(1)
    loads[2].wait()
    relayout(2)
    for copy in consts:
        copy.wait()
    tables()
    arrived_some(p_copy, 0, 1, 4)
    start(p_copy, p_own, 8, 1)
    p_own(0).wait()
    arrived_some(p_copy, 0, 4, 8)
    start(q_copy, q_own, 32, 0)
    arrived_some(p_copy, 1, 1, 4)
    start(p_copy, p_own, 8, 2)
    arrived(q_copy, q_own, 32, 0)
    middle(0)
    start(b_copy, b_own, 32, 0)
    p_own(1).wait()
    arrived_some(p_copy, 1, 4, 8)
    start(q_copy, q_own, 32, 1)
    arrived(b_copy, b_own, 32, 0)
    arrived_some(p_copy, 2, 1, 4)
    start(r_copy, r_own, 8, 0)
    p_own(2).wait()
    arrived_some(p_copy, 2, 4, 8)
    start(q_copy, q_own, 32, 2)
    arrived(q_copy, q_own, 32, 1)
    middle(1)
    start(b_copy, b_own, 32, 1)
    arrived(b_copy, b_own, 32, 1)
    arrived_some(r_copy, 0, 1, 4)
    start(r_copy, r_own, 8, 1)
    arrived(q_copy, q_own, 32, 2)
    middle(2)
    start(b_copy, b_own, 32, 2)
    r_own(0).wait()
    arrived_some(r_copy, 0, 4, 8)
    final(0)
    arrived(b_copy, b_own, 32, 2)
    arrived_some(r_copy, 1, 1, 4)
    start(r_copy, r_own, 8, 2)
    r_own(1).wait()
    arrived_some(r_copy, 1, 4, 8)
    final(1)
    arrived(r_copy, r_own, 8, 2)
    final(2)
    sent(p_copy, 8)
    sent(q_copy, 32)
    sent(b_copy, 32)
    sent(r_copy, 8)
    for c in range(CHUNKS):
        store(c).wait()


def solution(mesh):
    gdev, floc, twid = device_table(), local_table(), twiddle_table()

    def step(velocity):
        anywhere = pl.BlockSpec(memory_space=pl.ANY)
        tiles = pltpu.VMEM((CHUNKS, 256, 8, 128), F32)
        return pl.pallas_call(
            kernel,
            out_shape=jax.ShapeDtypeStruct(velocity.shape, F32),
            in_specs=[anywhere] * 4,
            out_specs=anywhere,
            scratch_shapes=[
                pltpu.VMEM((2, 6, 256, 256), F32),
                tiles,
                pltpu.VMEM((CHUNKS, 8, 32, 8, 128), F32),
                tiles,
                tiles,
                pltpu.VMEM((CHUNKS, 8, 32, 8, 128), F32),
                tiles,
                pltpu.VMEM((2, 6, 256, 256), F32),
                pltpu.VMEM((2, 512, 512), BF16),
                pltpu.VMEM((2, 256, 256), F32),
                pltpu.VMEM((16, 2, 8, 256), F32),
                pltpu.VMEM((2, 512, 512), BF16),
                pltpu.VMEM((2, 512, 512), BF16),
                pltpu.SemaphoreType.DMA((CHUNKS,)),
                pltpu.SemaphoreType.DMA((3,)),
                pltpu.SemaphoreType.DMA((CHUNKS,)),
                pltpu.SemaphoreType.DMA((CHUNKS, 8)),
                pltpu.SemaphoreType.DMA((CHUNKS, 8)),
                pltpu.SemaphoreType.DMA((CHUNKS, 32)),
                pltpu.SemaphoreType.DMA((CHUNKS, 32)),
                pltpu.SemaphoreType.DMA((CHUNKS, 32)),
                pltpu.SemaphoreType.DMA((CHUNKS, 32)),
                pltpu.SemaphoreType.DMA((CHUNKS, 8)),
                pltpu.SemaphoreType.DMA((CHUNKS, 8)),
            ],
            compiler_params=pltpu.CompilerParams(collective_id=0, has_side_effects=True, vmem_limit_bytes=56 * 2**20),
        )(velocity, jnp.asarray(gdev), jnp.asarray(floc), jnp.asarray(twid))

    return jax.shard_map(
        step, mesh=mesh, in_specs=(P(None, None, "gy", "gz"),), out_specs=P(None, None, "gy", "gz"), check_vma=False
    )
```

time: 694 us -> 171 us (0.25)
  waiting for transfers between devices: 613 us -> 0 us
  Pallas kernels: 0 us -> 164 us
  other arithmetic: 38 us -> 0 us
  matrix products: 21 us -> 0 us
  starting transfers between devices: 18.8 us -> 0 us
    ppermute x8 -> x0, waiting for transfers between devices: 613 us -> none  [swapped(): return lax.ppermute(block, axis, route)]
    pallas_call x0 -> x1, Pallas kernels: none -> 164 us  [step(): pl.pallas_call(kernel, out_shape=jax.ShapeDtypeStruct(velocity.shape, F32...]
    dot_general x8 -> x0, matrix products: 21 us -> none  [single(): return jnp.einsum(form, left, right, precision=lax.Precision.HIGHEST)]
    ppermute x8 -> x0, starting transfers between devices: 18.8 us -> none  [swapped(): return lax.ppermute(block, axis, route)]
    add x8 -> x0, other arithmetic: 18.4 us -> none  [butterfly(): mixed = own_block * flip + partner_block]
    another operation x8 -> x0, other arithmetic: 16.4 us -> none  [the longest x6 12.3 us: twist(): jnp.stack([real_part * cosine - imag_part * sine, real_part * sine + imag...]
  transfers between devices with their start and end apart: 8 -> 0, of which waited for: 8 -> 0; matrix products, arithmetic and copies ran while one was open for 0% -> 0% of each run, Pallas kernels for 0% -> 0%
where the time goes in v1:
time: 171 us; the launch traced here: 168 us
  Pallas kernels  164 us (96%)
  local copies, waits for them, and re-layouts  3.76 us (2%)
    pallas_call x1, Pallas kernels, step(): pl.pallas_call(kernel, out_shape=jax.ShapeDtypeStruct(velocity.shape, F32...  164 us
    unnamed x1, local copies, waits for them, and re-layouts  3.76 us

profile of v1, /device:TPU:8, one launch (start us, length us, event | category | flops | bytes accessed | tf_op | source)
XLA Modules:
  0.0 168.1 jit_solution(13902490492568480729)
XLA Ops:
  0.0 164.3 %shard_map.46 = f32[2,6,256,256]{3,2,1,0:T(8,128)} custom-call(f32[2,6,256,256]{3,2,1,0:T(8,128)} %x_hbm.1, bf16[2,512,512]{2,1,0:T(8,128)(2,1)} %constant.6.clone.gdev_hbm, f32[2,256,256]{2,1,0:T(8,128)} %constant.7.clone.floc_hbm, f32[16,2,8,256]{3,2,1,0:T(8,128)} %constant.8.clone.twid_hbm), custom_call_target="tpu_custom_call" | custom-call | tf_op jit(solution)/shard_map/pallas_call | solution.py:288
  164.4 3.8 %copy.6 = f32[2,6,256,256]{3,2,1,0:T(8,128)} copy(f32[2,6,256,256]{3,2,1,0:T(8,128)} %shard_map.46) | data formatting | bytes 6291456

commit v2 on v1

v2 whole, which is shorter than its diff:
```python
import jax
import jax.numpy as jnp
import ml_dtypes
import numpy as np
from jax import lax
from jax.experimental import pallas as pl
from jax.experimental.pallas import tpu as pltpu
from jax.sharding import PartitionSpec as P

MESH = pl.DeviceIdType.MESH
F32 = jnp.float32
BF16 = jnp.bfloat16
CHUNKS = 3
NZD = 8


def reversed_bits(value):
    return int(format(value, "04b")[::-1], 2)


def split_host(table):
    high = table.astype(np.float32).astype(ml_dtypes.bfloat16)
    low = (table - high.astype(np.float64)).astype(ml_dtypes.bfloat16)
    return np.stack([high, low])


def device_table():
    index = np.arange(256)
    q, z = index // NZD, index % NZD
    core, y, x = q // 16, q // 4 % 4, q % 4
    cz, cy = y % 2 * 8 + z, y // 2 * 8 + x * 2 + core
    kz = np.array([reversed_bits(c) for c in cz])
    ky = np.array([reversed_bits(c) for c in cy])
    phase = -2.0 * np.pi * ((kz[:, None] * cz[None, :] + ky[:, None] * cy[None, :]) % 16) / 16
    c, s = np.cos(phase), np.sin(phase)
    return split_host(np.block([[c, -s], [s, c]]))


def local_order():
    half, z, row = np.meshgrid(np.arange(2), np.arange(8), np.arange(16), indexing="ij")
    return (z * 32 + half * 16 + row).reshape(256)


def local_table(order):
    index = np.arange(256)
    phase = -2.0 * np.pi * ((index[:, None] * order[None, :]) % 256) / 256
    return (np.stack([np.cos(phase), np.sin(phase)]) / 64).astype(np.float32)


def twiddle_table(order):
    frequency = np.array([reversed_bits(c) for c in range(16)])
    phase = -2.0 * np.pi * ((frequency[:, None] * order[None, :]) % 4096) / 4096
    both = np.stack([np.cos(phase), np.sin(phase)], axis=1).astype(np.float32)
    return np.repeat(both[:, :, None, :], 8, axis=2)


def split(values):
    high = values.astype(BF16)
    return high, (values - high.astype(F32)).astype(BF16)


def mm(left, right):
    return jnp.dot(left, right, preferred_element_type=F32)


def kernel(
    x_hbm, gdev_hbm, floc_hbm, twid_hbm, o_hbm,
    xin, send_p, recv_p, mid_in, mid_out, recv_q, recv_r, part, out, gdev, floc, twid, ytab, ztab,
    in_sem, const_sem, out_sem, psend, precv, qsend, qrecv, bsend, brecv, rsend, rrecv,
):
    gz, gy = lax.axis_index("gz"), lax.axis_index("gy")
    yl, z = gz // 8, gz % 8
    yh, xc, co = gy // 8, gy // 2 % 4, gy % 2
    yc = yh * 2 + yl
    row = yc * 4 + xc
    q = co * 16 + row

    def z_partner(t):
        zt = (z + t) % 8
        return zt, (yl * 8 + zt, gy)

    def q_partner(t, dc):
        a, b = t // 4, t % 4
        dy, dx = a + co * (b - a), b + co * (a - b)
        y2, x2, c2 = (yc + dy) % 4, (xc + dx) % 4, (co + dc) % 2
        return y2 * 4 + x2, (y2 % 2 * 8 + z, y2 // 2 * 8 + x2 * 2 + c2), (dy * 4 + dx) * 2 + dc

    loads = [pltpu.make_async_copy(x_hbm.at[:, pl.ds(2 * c, 2)], xin.at[:, pl.ds(2 * c, 2)], in_sem.at[c]) for c in range(CHUNKS)]
    consts = [
        pltpu.make_async_copy(floc_hbm, floc, const_sem.at[0]),
        pltpu.make_async_copy(twid_hbm, twid, const_sem.at[1]),
        pltpu.make_async_copy(gdev_hbm, gdev, const_sem.at[2]),
    ]
    for copy in loads + consts:
        copy.start()

    barrier = pltpu.get_barrier_semaphore()

    @pl.loop(1, 8)
    def _(t):
        pl.semaphore_signal(barrier, inc=1, device_id=z_partner(t)[1], device_id_type=MESH)

    @pl.loop(1, 32)
    def _(t):
        pl.semaphore_signal(barrier, inc=1, device_id=q_partner(t // 2, t % 2)[1], device_id_type=MESH)

    def relayout(c, half):
        flat = send_p.at[c, half].reshape(1024, 128)
        for p in range(2):
            for r in range(2):
                for h in range(2):
                    for zt in range(8):
                        first = zt * 32 + half * 16
                        flat[pl.ds(zt * 128 + p * 4 + r * 2 + h, 16, stride=8), :] = xin[r, 2 * c + p, first : first + 16, h * 128 : h * 128 + 128]

    def remote(source, target, send_sem, recv_sem, device):
        return pltpu.make_async_remote_copy(source, target, send_sem, recv_sem, device_id=device, device_id_type=MESH)

    def p_copy(c, half, t):
        zt, device = z_partner(t)
        return remote(send_p.at[c, half, zt], recv_p.at[c, half, z], psend.at[c, half, t], precv.at[c, half, t], device)

    def p_own(c, half):
        return pltpu.make_async_copy(send_p.at[c, half, z], recv_p.at[c, half, z], precv.at[c, half, 0])

    def r_copy(c, half, t):
        zt, device = z_partner(t)
        return remote(recv_q.at[c, half, zt], recv_r.at[c, half, z], rsend.at[c, half, t], rrecv.at[c, half, t], device)

    def r_own(c, half):
        return pltpu.make_async_copy(recv_q.at[c, half, z], recv_r.at[c, half, z], rrecv.at[c, half, 0])

    def q_copy(c, t, dc):
        there, device, slot = q_partner(t, dc)
        half = (co + dc) % 2
        return remote(recv_p.at[c, half, :, there], mid_in.at[c, q], qsend.at[c, slot], qrecv.at[c, slot], device)

    def q_own(c):
        return pltpu.make_async_copy(recv_p.at[c, co, :, row], mid_in.at[c, q], qrecv.at[c, 0])

    def b_copy(c, t, dc):
        there, device, slot = q_partner(t, dc)
        half = (co + dc) % 2
        return remote(mid_out.at[c, half * 16 + there], recv_q.at[c, co, :, row], bsend.at[c, slot], brecv.at[c, slot], device)

    def b_own(c):
        return pltpu.make_async_copy(mid_out.at[c, q], recv_q.at[c, co, :, row], brecv.at[c, 0])

    def start_z(copy, own, c, half):
        own(c, half).start()

        @pl.loop(1, 8)
        def _(t):
            copy(c, half, t).start()

    def wait_z(copy, own, c, half):
        own(c, half).wait()

        @pl.loop(1, 8)
        def _(t):
            copy(c, half, t).wait_recv()

    def start_q(c, half):
        dc = (half + co) % 2

        @pl.loop(1, 8)
        def _(t):
            q_copy(c, t, dc).start()
            q_copy(c, 16 - t, dc).start()

        q_copy(c, 8, dc).start()

        @pl.when(dc == 0)
        def _():
            q_own(c).start()

        @pl.when(dc == 1)
        def _():
            q_copy(c, 0, 1).start()

    def wait_q(c):
        q_own(c).wait()

        @pl.loop(1, 32)
        def _(t):
            q_copy(c, t // 2, t % 2).wait_recv()

    def start_b(c):
        @pl.loop(1, 8)
        def _(t):
            for dc in range(2):
                b_copy(c, t, dc).start()
                b_copy(c, 16 - t, dc).start()

        b_copy(c, 8, 0).start()
        b_copy(c, 8, 1).start()
        b_copy(c, 0, 1).start()
        b_own(c).start()

    def wait_b(c, half):
        dc = (half + co) % 2

        @pl.when(dc == 0)
        def _():
            b_own(c).wait()

        @pl.when(dc == 1)
        def _():
            b_copy(c, 0, 1).wait_recv()

        @pl.loop(1, 16)
        def _(t):
            b_copy(c, t, dc).wait_recv()

    def sent():
        for c in range(CHUNKS):

            @pl.loop(1, 8)
            def _(t):
                for half in range(2):
                    p_copy(c, half, t).wait_send()
                    r_copy(c, half, t).wait_send()

            @pl.loop(1, 32)
            def _(t):
                q_copy(c, t // 2, t % 2).wait_send()
                b_copy(c, t // 2, t % 2).wait_send()

    def read_rows(ref, count):
        flat = ref.reshape(count * 8, 128)
        rows = [
            jnp.concatenate([flat[pl.ds(p * 4 + r * 2 + h, count, stride=8), :] for p in range(2) for h in range(2)], axis=1)
            for r in range(2)
        ]
        return jnp.concatenate(rows, axis=0)

    def middle(c):
        xh, xl = split(read_rows(mid_in.at[c], 256))
        y = mm(gdev[0], xh) + mm(gdev[0], xl) + mm(gdev[1], xh)
        flat = mid_out.at[c].reshape(2048, 128)
        for p in range(2):
            for r in range(2):
                for h in range(2):
                    flat[pl.ds(p * 4 + r * 2 + h, 256, stride=8), :] = y[r * 256 : r * 256 + 256, (p * 2 + h) * 128 : (p * 2 + h) * 128 + 128]

    def twisted(axis, position):
        fr, fi = floc[axis, 0], floc[axis, 1]
        tc, ts = twid[axis, position, 0, 0:1], twid[axis, position, 1, 0:1]
        return fr * tc - fi * ts, fr * ts + fi * tc

    def tables():
        a, b = twisted(0, gy)
        for half in range(2):
            ah, bh = a[:, half * 128 : half * 128 + 128], b[:, half * 128 : half * 128 + 128]
            full = jnp.concatenate([jnp.concatenate([ah, -bh], axis=1), jnp.concatenate([bh, ah], axis=1)], axis=0)
            ytab[half, 0], ytab[half, 1] = split(full)
        a, b = twisted(1, gz)
        a, b = a.T, b.T
        full = jnp.concatenate([jnp.concatenate([a, b], axis=1), jnp.concatenate([-b, a], axis=1)], axis=0)
        ztab[0], ztab[1] = split(full)

    def store(c):
        return pltpu.make_async_copy(out.at[:, pl.ds(2 * c, 2)], o_hbm.at[:, pl.ds(2 * c, 2)], out_sem.at[c])

    def along_y(c, half):
        xh, xl = split(read_rows(recv_r.at[c, half], 128))
        return mm(ytab[half, 0], xh) + mm(ytab[half, 0], xl) + mm(ytab[half, 1], xh)

    def final_first(c):
        part[...] = along_y(c, 0)

    def final_second(c):
        u = part[...] + along_y(c, 1)
        for p in range(2):
            w = jnp.concatenate([u[:256, p * 256 : p * 256 + 256], u[256:, p * 256 : p * 256 + 256]], axis=1)
            wh, wl = split(w)
            v = mm(wh, ztab[0]) + mm(wl, ztab[0]) + mm(wh, ztab[1])
            out[0, 2 * c + p] = v[:, :256]
            out[1, 2 * c + p] = v[:, 256:]
        store(c).start()

    loads[0].wait()
    relayout(0, 0)
    pl.semaphore_wait(barrier, 38)
    start_z(p_copy, p_own, 0, 0)
    relayout(0, 1)
    start_z(p_copy, p_own, 0, 1)
    for c in range(1, CHUNKS):
        loads[c].wait()
        relayout(c, 0)
        relayout(c, 1)
    for copy in consts:
        copy.wait()
    tables()
    wait_z(p_copy, p_own, 0, 0)
    start_q(0, 0)
    start_z(p_copy, p_own, 1, 0)
    wait_z(p_copy, p_own, 0, 1)
    start_q(0, 1)
    start_z(p_copy, p_own, 1, 1)
    wait_q(0)
    middle(0)
    start_b(0)
    wait_z(p_copy, p_own, 1, 0)
    start_q(1, 0)
    start_z(p_copy, p_own, 2, 0)
    wait_z(p_copy, p_own, 1, 1)
    start_q(1, 1)
    start_z(p_copy, p_own, 2, 1)
    wait_b(0, 0)
    start_z(r_copy, r_own, 0, 0)
    wait_b(0, 1)
    start_z(r_copy, r_own, 0, 1)
    wait_q(1)
    middle(1)
    start_b(1)
    wait_z(p_copy, p_own, 2, 0)
    start_q(2, 0)
    wait_z(p_copy, p_own, 2, 1)
    start_q(2, 1)
    wait_b(1, 0)
    start_z(r_copy, r_own, 1, 0)
    wait_b(1, 1)
    start_z(r_copy, r_own, 1, 1)
    wait_q(2)
    middle(2)
    start_b(2)
    wait_z(r_copy, r_own, 0, 0)
    final_first(0)
    wait_z(r_copy, r_own, 0, 1)
    final_second(0)
    wait_b(2, 0)
    start_z(r_copy, r_own, 2, 0)
    wait_b(2, 1)
    start_z(r_copy, r_own, 2, 1)
    wait_z(r_copy, r_own, 1, 0)
    final_first(1)
    wait_z(r_copy, r_own, 1, 1)
    final_second(1)
    wait_z(r_copy, r_own, 2, 0)
    final_first(2)
    wait_z(r_copy, r_own, 2, 1)
    final_second(2)
    sent()
    for c in range(CHUNKS):
        store(c).wait()


def solution(mesh):
    gdev = device_table()
    orders = (local_order(), np.arange(256))
    floc = np.stack([local_table(order) for order in orders])
    twid = np.stack([twiddle_table(order) for order in orders])

    def step(velocity):
        anywhere = pl.BlockSpec(memory_space=pl.ANY)
        halves = pltpu.VMEM((CHUNKS, 2, 8, 16, 8, 128), F32)
        middles = pltpu.VMEM((CHUNKS, 32, 8, 8, 128), F32)
        return pl.pallas_call(
            kernel,
            out_shape=jax.ShapeDtypeStruct(velocity.shape, F32),
            in_specs=[anywhere] * 4,
            out_specs=anywhere,
            scratch_shapes=[
                pltpu.VMEM((2, 6, 256, 256), F32),
                halves,
                halves,
                middles,
                middles,
                halves,
                halves,
                pltpu.VMEM((512, 512), F32),
                pltpu.VMEM((2, 6, 256, 256), F32),
                pltpu.VMEM((2, 512, 512), BF16),
                pltpu.VMEM((2, 2, 256, 256), F32),
                pltpu.VMEM((2, 16, 2, 8, 256), F32),
                pltpu.VMEM((2, 2, 512, 256), BF16),
                pltpu.VMEM((2, 512, 512), BF16),
                pltpu.SemaphoreType.DMA((CHUNKS,)),
                pltpu.SemaphoreType.DMA((3,)),
                pltpu.SemaphoreType.DMA((CHUNKS,)),
                pltpu.SemaphoreType.DMA((CHUNKS, 2, 8)),
                pltpu.SemaphoreType.DMA((CHUNKS, 2, 8)),
                pltpu.SemaphoreType.DMA((CHUNKS, 32)),
                pltpu.SemaphoreType.DMA((CHUNKS, 32)),
                pltpu.SemaphoreType.DMA((CHUNKS, 32)),
                pltpu.SemaphoreType.DMA((CHUNKS, 32)),
                pltpu.SemaphoreType.DMA((CHUNKS, 2, 8)),
                pltpu.SemaphoreType.DMA((CHUNKS, 2, 8)),
            ],
            compiler_params=pltpu.CompilerParams(collective_id=0, has_side_effects=True, vmem_limit_bytes=56 * 2**20),
        )(velocity, jnp.asarray(gdev), jnp.asarray(floc), jnp.asarray(twid))

    return jax.shard_map(
        step, mesh=mesh, in_specs=(P(None, None, "gy", "gz"),), out_specs=P(None, None, "gy", "gz"), check_vma=False
    )
```

time: 171 us -> 162 us (0.947); the launches traced: 168 us -> 162 us
  Pallas kernels: 164 us -> 158 us
    pallas_call x1, Pallas kernels: 164 us -> 158 us  [step(): pl.pallas_call(kernel, out_shape=jax.ShapeDtypeStruct(velocity.shape, F32...]
where the time goes in v2:
time: 162 us
  Pallas kernels  158 us (98%)
  local copies, waits for them, and re-layouts  3.76 us (2%)
    pallas_call x1, Pallas kernels, step(): pl.pallas_call(kernel, out_shape=jax.ShapeDtypeStruct(velocity.shape, F32...  158 us
    unnamed x1, local copies, waits for them, and re-layouts  3.76 us

profile of v2, /device:TPU:8, one launch (start us, length us, event | category | flops | bytes accessed | tf_op | source)
XLA Modules:
  0.0 161.7 jit_solution(12411219092487115309)
XLA Ops:
  0.0 157.9 %shard_map.46 = f32[2,6,256,256]{3,2,1,0:T(8,128)} custom-call(f32[2,6,256,256]{3,2,1,0:T(8,128)} %x_hbm.1, bf16[2,512,512]{2,1,0:T(8,128)(2,1)} %constant.6.clone.gdev_hbm, f32[2,2,256,256]{3,2,1,0:T(8,128)} %constant.7.clone.floc_hbm, f32[2,16,2,8,256]{4,3,2,1,0:T(8,128)} %constant.8.clone.twid_hbm), custom_call_target="tpu_custom_call" | custom-call | tf_op jit(solution)/shard_map/pallas_call | solution.py:359
  158.0 3.8 %copy.6 = f32[2,6,256,256]{3,2,1,0:T(8,128)} copy(f32[2,6,256,256]{3,2,1,0:T(8,128)} %shard_map.46) | data formatting | bytes 6291456

commit v3 on v2

--- a/solution.py
+++ b/solution.py
@@ -64,9 +64,9 @@
 
 
 def kernel(
-    x_hbm, gdev_hbm, floc_hbm, twid_hbm, o_hbm,
-    xin, send_p, recv_p, mid_in, mid_out, recv_q, recv_r, part, out, gdev, floc, twid, ytab, ztab,
-    in_sem, const_sem, out_sem, psend, precv, qsend, qrecv, bsend, brecv, rsend, rrecv,
+    x_hbm, gdev_hbm, floc_hbm, twid_hbm, out,
+    xin, send_p, recv_p, mid_in, mid_out, recv_q, recv_r, part, gdev, floc, twid, ytab, ztab,
+    in_sem, const_sem, psend, precv, qsend, qrecv, bsend, brecv, rsend, rrecv,
 ):
     gz, gy = lax.axis_index("gz"), lax.axis_index("gy")
     yl, z = gz // 8, gz % 8
@@ -212,19 +212,16 @@
         def _(t):
             b_copy(c, t, dc).wait_recv()
 
-    def sent():
-        for c in range(CHUNKS):
-
-            @pl.loop(1, 8)
-            def _(t):
-                for half in range(2):
-                    p_copy(c, half, t).wait_send()
-                    r_copy(c, half, t).wait_send()
-
-            @pl.loop(1, 32)
-            def _(t):
-                q_copy(c, t // 2, t % 2).wait_send()
-                b_copy(c, t // 2, t % 2).wait_send()
+    def sent_z(copy, c):
+        @pl.loop(1, 8)
+        def _(t):
+            for half in range(2):
+                copy(c, half, t).wait_send()
+
+    def sent_q(copy, c):
+        @pl.loop(1, 32)
+        def _(t):
+            copy(c, t // 2, t % 2).wait_send()
 
     def read_rows(ref, count):
         flat = ref.reshape(count * 8, 128)
@@ -259,9 +256,6 @@
         full = jnp.concatenate([jnp.concatenate([a, b], axis=1), jnp.concatenate([-b, a], axis=1)], axis=0)
         ztab[0], ztab[1] = split(full)
 
-    def store(c):
-        return pltpu.make_async_copy(out.at[:, pl.ds(2 * c, 2)], o_hbm.at[:, pl.ds(2 * c, 2)], out_sem.at[c])
-
     def along_y(c, half):
         xh, xl = split(read_rows(recv_r.at[c, half], 128))
         return mm(ytab[half, 0], xh) + mm(ytab[half, 0], xl) + mm(ytab[half, 1], xh)
@@ -277,7 +271,6 @@
             v = mm(wh, ztab[0]) + mm(wl, ztab[0]) + mm(wh, ztab[1])
             out[0, 2 * c + p] = v[:, :256]
             out[1, 2 * c + p] = v[:, 256:]
-        store(c).start()
 
     loads[0].wait()
     relayout(0, 0)
@@ -333,17 +326,22 @@
     start_z(r_copy, r_own, 2, 0)
     wait_b(2, 1)
     start_z(r_copy, r_own, 2, 1)
+    for c in range(CHUNKS):
+        sent_z(p_copy, c)
+        sent_q(q_copy, c)
     wait_z(r_copy, r_own, 1, 0)
     final_first(1)
+    for c in range(CHUNKS):
+        sent_q(b_copy, c)
     wait_z(r_copy, r_own, 1, 1)
     final_second(1)
+    sent_z(r_copy, 0)
+    sent_z(r_copy, 1)
     wait_z(r_copy, r_own, 2, 0)
     final_first(2)
     wait_z(r_copy, r_own, 2, 1)
     final_second(2)
-    sent()
-    for c in range(CHUNKS):
-        store(c).wait()
+    sent_z(r_copy, 2)
 
 
 def solution(mesh):
@@ -358,9 +356,9 @@
         middles = pltpu.VMEM((CHUNKS, 32, 8, 8, 128), F32)
         return pl.pallas_call(
             kernel,
-            out_shape=jax.ShapeDtypeStruct(velocity.shape, F32),
-            in_specs=[anywhere] * 4,
-            out_specs=anywhere,
+            out_shape=pltpu.VMEM(velocity.shape, F32),
+            in_specs=[pl.BlockSpec(memory_space=pltpu.HBM)] * 4,
+            out_specs=pl.BlockSpec(memory_space=pltpu.VMEM),
             scratch_shapes=[
                 pltpu.VMEM((2, 6, 256, 256), F32),
                 halves,
@@ -370,7 +368,6 @@
                 halves,
                 halves,
                 pltpu.VMEM((512, 512), F32),
-                pltpu.VMEM((2, 6, 256, 256), F32),
                 pltpu.VMEM((2, 512, 512), BF16),
                 pltpu.VMEM((2, 2, 256, 256), F32),
                 pltpu.VMEM((2, 16, 2, 8, 256), F32),
@@ -378,7 +375,6 @@
                 pltpu.VMEM((2, 512, 512), BF16),
                 pltpu.SemaphoreType.DMA((CHUNKS,)),
                 pltpu.SemaphoreType.DMA((3,)),
-                pltpu.SemaphoreType.DMA((CHUNKS,)),
                 pltpu.SemaphoreType.DMA((CHUNKS, 2, 8)),
                 pltpu.SemaphoreType.DMA((CHUNKS, 2, 8)),
                 pltpu.SemaphoreType.DMA((CHUNKS, 32)),
@@ -388,8 +384,8 @@
                 pltpu.SemaphoreType.DMA((CHUNKS, 2, 8)),
                 pltpu.SemaphoreType.DMA((CHUNKS, 2, 8)),
             ],
-            compiler_params=pltpu.CompilerParams(collective_id=0, has_side_effects=True, vmem_limit_bytes=56 * 2**20),
-        )(velocity, jnp.asarray(gdev), jnp.asarray(floc), jnp.asarray(twid))
+            compiler_params=pltpu.CompilerParams(collective_id=0, has_side_effects=True, vmem_limit_bytes=40 * 2**20),
+        )(*[pltpu.with_memory_space_constraint(a, pltpu.HBM) for a in (velocity, jnp.asarray(gdev), jnp.asarray(floc), jnp.asarray(twid))])
 
     return jax.shard_map(
         step, mesh=mesh, in_specs=(P(None, None, "gy", "gz"),), out_specs=P(None, None, "gy", "gz"), check_vma=False

time: 162 us -> 157 us (0.969)
  Pallas kernels: 158 us -> 155 us
  local copies, waits for them, and re-layouts: 3.76 us -> 1.67 us
    pallas_call x1, Pallas kernels: 158 us -> 155 us  [step(): pl.pallas_call(kernel, out_shape=pltpu.VMEM(velocity.shape, F32), in_spec...]
    unnamed x1, local copies, waits for them, and re-layouts: 3.76 us -> 1.67 us
where the time goes in v3:
time: 157 us
  Pallas kernels  155 us (99%)
  local copies, waits for them, and re-layouts  1.67 us (1%)
    pallas_call x1, Pallas kernels, step(): pl.pallas_call(kernel, out_shape=pltpu.VMEM(velocity.shape, F32), in_spec...  155 us

profile of v3, /device:TPU:8, one launch (start us, length us, event | category | flops | bytes accessed | tf_op | source)
XLA Modules:
  0.0 157.1 jit_solution(2652307748026261381)
XLA Ops:
  0.0 155.4 %shard_map.46 = f32[2,6,256,256]{3,2,1,0:T(8,128)S(1)} custom-call(f32[2,6,256,256]{3,2,1,0:T(8,128)} %x_hbm.1, bf16[2,512,512]{2,1,0:T(8,128)(2,1)} %constant.6.clone.gdev_hbm, f32[2,2,256,256]{3,2,1,0:T(8,128)} %constant.7.clone.floc_hbm, f32[2,16,2,8,256]{4,3,2,1,0:T(8,128)} %constant.8.clone.twid_hbm), custom_call_target="tpu_custom_call" | custom-call | tf_op jit(solution)/shard_map/pallas_call | solution.py:357
  155.4 1.7 %copy.6 = f32[2,6,256,256]{3,2,1,0:T(8,128)} copy(f32[2,6,256,256]{3,2,1,0:T(8,128)S(1)} %shard_map.46) | data formatting | bytes 6291456

commit v4 on v3

--- a/solution.py
+++ b/solution.py
@@ -83,7 +83,7 @@
         a, b = t // 4, t % 4
         dy, dx = a + co * (b - a), b + co * (a - b)
         y2, x2, c2 = (yc + dy) % 4, (xc + dx) % 4, (co + dc) % 2
-        return y2 * 4 + x2, (y2 % 2 * 8 + z, y2 // 2 * 8 + x2 * 2 + c2), (dy * 4 + dx) * 2 + dc
+        return y2 * 4 + x2, (y2 % 2 * 8 + z, y2 // 2 * 8 + x2 * 2 + c2)
 
     loads = [pltpu.make_async_copy(x_hbm.at[:, pl.ds(2 * c, 2)], xin.at[:, pl.ds(2 * c, 2)], in_sem.at[c]) for c in range(CHUNKS)]
     consts = [
@@ -118,33 +118,33 @@
 
     def p_copy(c, half, t):
         zt, device = z_partner(t)
-        return remote(send_p.at[c, half, zt], recv_p.at[c, half, z], psend.at[c, half, t], precv.at[c, half, t], device)
+        return remote(send_p.at[c, half, zt], recv_p.at[c, half, z], psend.at[c], precv.at[c, half], device)
 
     def p_own(c, half):
-        return pltpu.make_async_copy(send_p.at[c, half, z], recv_p.at[c, half, z], precv.at[c, half, 0])
+        return pltpu.make_async_copy(send_p.at[c, half, z], recv_p.at[c, half, z], precv.at[c, half])
 
     def r_copy(c, half, t):
         zt, device = z_partner(t)
-        return remote(recv_q.at[c, half, zt], recv_r.at[c, half, z], rsend.at[c, half, t], rrecv.at[c, half, t], device)
+        return remote(recv_q.at[c, half, zt], recv_r.at[c, half, z], rsend.at[c], rrecv.at[c, half], device)
 
     def r_own(c, half):
-        return pltpu.make_async_copy(recv_q.at[c, half, z], recv_r.at[c, half, z], rrecv.at[c, half, 0])
+        return pltpu.make_async_copy(recv_q.at[c, half, z], recv_r.at[c, half, z], rrecv.at[c, half])
 
     def q_copy(c, t, dc):
-        there, device, slot = q_partner(t, dc)
+        there, device = q_partner(t, dc)
         half = (co + dc) % 2
-        return remote(recv_p.at[c, half, :, there], mid_in.at[c, q], qsend.at[c, slot], qrecv.at[c, slot], device)
+        return remote(recv_p.at[c, half, :, there], mid_in.at[c, q], qsend.at[c], qrecv.at[c], device)
 
     def q_own(c):
-        return pltpu.make_async_copy(recv_p.at[c, co, :, row], mid_in.at[c, q], qrecv.at[c, 0])
+        return pltpu.make_async_copy(recv_p.at[c, co, :, row], mid_in.at[c, q], qrecv.at[c])
 
     def b_copy(c, t, dc):
-        there, device, slot = q_partner(t, dc)
+        there, device = q_partner(t, dc)
         half = (co + dc) % 2
-        return remote(mid_out.at[c, half * 16 + there], recv_q.at[c, co, :, row], bsend.at[c, slot], brecv.at[c, slot], device)
+        return remote(mid_out.at[c, half * 16 + there], recv_q.at[c, co, :, row], bsend.at[c], brecv.at[c, co], device)
 
     def b_own(c):
-        return pltpu.make_async_copy(mid_out.at[c, q], recv_q.at[c, co, :, row], brecv.at[c, 0])
+        return pltpu.make_async_copy(mid_out.at[c, q], recv_q.at[c, co, :, row], brecv.at[c, co])
 
     def start_z(copy, own, c, half):
         own(c, half).start()
@@ -153,12 +153,8 @@
         def _(t):
             copy(c, half, t).start()
 
-    def wait_z(copy, own, c, half):
-        own(c, half).wait()
-
-        @pl.loop(1, 8)
-        def _(t):
-            copy(c, half, t).wait_recv()
+    def wait_bytes(ref, sem):
+        pltpu.make_async_copy(ref, ref, sem).wait()
 
     def start_q(c, half):
         dc = (half + co) % 2
@@ -177,13 +173,6 @@
         @pl.when(dc == 1)
         def _():
             q_copy(c, 0, 1).start()
-
-    def wait_q(c):
-        q_own(c).wait()
-
-        @pl.loop(1, 32)
-        def _(t):
-            q_copy(c, t // 2, t % 2).wait_recv()
 
     def start_b(c):
         @pl.loop(1, 8)
@@ -196,32 +185,6 @@
         b_copy(c, 8, 1).start()
         b_copy(c, 0, 1).start()
         b_own(c).start()
-
-    def wait_b(c, half):
-        dc = (half + co) % 2
-
-        @pl.when(dc == 0)
-        def _():
-            b_own(c).wait()
-
-        @pl.when(dc == 1)
-        def _():
-            b_copy(c, 0, 1).wait_recv()
-
-        @pl.loop(1, 16)
-        def _(t):
-            b_copy(c, t, dc).wait_recv()
-
-    def sent_z(copy, c):
-        @pl.loop(1, 8)
-        def _(t):
-            for half in range(2):
-                copy(c, half, t).wait_send()
-
-    def sent_q(copy, c):
-        @pl.loop(1, 32)
-        def _(t):
-            copy(c, t // 2, t % 2).wait_send()
 
     def read_rows(ref, count):
         flat = ref.reshape(count * 8, 128)
@@ -256,21 +219,23 @@
         full = jnp.concatenate([jnp.concatenate([a, b], axis=1), jnp.concatenate([-b, a], axis=1)], axis=0)
         ztab[0], ztab[1] = split(full)
 
-    def along_y(c, half):
-        xh, xl = split(read_rows(recv_r.at[c, half], 128))
-        return mm(ytab[half, 0], xh) + mm(ytab[half, 0], xl) + mm(ytab[half, 1], xh)
+    def transformed(c, half):
+        flat = recv_r.at[c, half].reshape(1024, 128)
+        rows = [jnp.concatenate([flat[pl.ds(p * 4 + s, 128, stride=8), :] for s in range(4)], axis=1) for p in range(2)]
+        xh, xl = split(jnp.concatenate(rows, axis=0))
+        v = mm(xh, ztab[0]) + mm(xl, ztab[0]) + mm(xh, ztab[1])
+        planes = [jnp.concatenate([v[p * 128 : p * 128 + 128, :256], v[p * 128 : p * 128 + 128, 256:]], axis=0) for p in range(2)]
+        vh, vl = split(jnp.concatenate(planes, axis=1))
+        return mm(ytab[half, 0], vh) + mm(ytab[half, 0], vl) + mm(ytab[half, 1], vh)
 
     def final_first(c):
-        part[...] = along_y(c, 0)
+        part[...] = transformed(c, 0)
 
     def final_second(c):
-        u = part[...] + along_y(c, 1)
+        u = part[...] + transformed(c, 1)
         for p in range(2):
-            w = jnp.concatenate([u[:256, p * 256 : p * 256 + 256], u[256:, p * 256 : p * 256 + 256]], axis=1)
-            wh, wl = split(w)
-            v = mm(wh, ztab[0]) + mm(wl, ztab[0]) + mm(wh, ztab[1])
-            out[0, 2 * c + p] = v[:, :256]
-            out[1, 2 * c + p] = v[:, 256:]
+            for r in range(2):
+                out[r, 2 * c + p] = u[r * 256 : r * 256 + 256, p * 256 : p * 256 + 256]
 
     loads[0].wait()
     relayout(0, 0)
@@ -285,63 +250,63 @@
     for copy in consts:
         copy.wait()
     tables()
-    wait_z(p_copy, p_own, 0, 0)
+    wait_bytes(recv_p.at[0, 0], precv.at[0, 0])
     start_q(0, 0)
     start_z(p_copy, p_own, 1, 0)
-    wait_z(p_copy, p_own, 0, 1)
+    wait_bytes(recv_p.at[0, 1], precv.at[0, 1])
     start_q(0, 1)
     start_z(p_copy, p_own, 1, 1)
-    wait_q(0)
+    wait_bytes(mid_in.at[0], qrecv.at[0])
     middle(0)
     start_b(0)
-    wait_z(p_copy, p_own, 1, 0)
+    wait_bytes(recv_p.at[1, 0], precv.at[1, 0])
     start_q(1, 0)
     start_z(p_copy, p_own, 2, 0)
-    wait_z(p_copy, p_own, 1, 1)
+    wait_bytes(recv_p.at[1, 1], precv.at[1, 1])
     start_q(1, 1)
     start_z(p_copy, p_own, 2, 1)
-    wait_b(0, 0)
+    wait_bytes(recv_q.at[0, 0], brecv.at[0, 0])
     start_z(r_copy, r_own, 0, 0)
-    wait_b(0, 1)
+    wait_bytes(recv_q.at[0, 1], brecv.at[0, 1])
     start_z(r_copy, r_own, 0, 1)
-    wait_q(1)
+    wait_bytes(mid_in.at[1], qrecv.at[1])
     middle(1)
     start_b(1)
-    wait_z(p_copy, p_own, 2, 0)
+    wait_bytes(recv_p.at[2, 0], precv.at[2, 0])
     start_q(2, 0)
-    wait_z(p_copy, p_own, 2, 1)
+    wait_bytes(recv_p.at[2, 1], precv.at[2, 1])
     start_q(2, 1)
-    wait_b(1, 0)
+    wait_bytes(recv_q.at[1, 0], brecv.at[1, 0])
     start_z(r_copy, r_own, 1, 0)
-    wait_b(1, 1)
+    wait_bytes(recv_q.at[1, 1], brecv.at[1, 1])
     start_z(r_copy, r_own, 1, 1)
-    wait_q(2)
+    wait_bytes(mid_in.at[2], qrecv.at[2])
     middle(2)
     start_b(2)
-    wait_z(r_copy, r_own, 0, 0)
+    wait_bytes(recv_r.at[0, 0], rrecv.at[0, 0])
     final_first(0)
-    wait_z(r_copy, r_own, 0, 1)
+    wait_bytes(recv_r.at[0, 1], rrecv.at[0, 1])
     final_second(0)
-    wait_b(2, 0)
+    wait_bytes(recv_q.at[2, 0], brecv.at[2, 0])
     start_z(r_copy, r_own, 2, 0)
-    wait_b(2, 1)
+    wait_bytes(recv_q.at[2, 1], brecv.at[2, 1])
     start_z(r_copy, r_own, 2, 1)
     for c in range(CHUNKS):
-        sent_z(p_copy, c)
-        sent_q(q_copy, c)
-    wait_z(r_copy, r_own, 1, 0)
+        wait_bytes(send_p.at[c, :, pl.ds(0, 7)], psend.at[c])
+        wait_bytes(mid_in.at[c, pl.ds(0, 31)], qsend.at[c])
+    wait_bytes(recv_r.at[1, 0], rrecv.at[1, 0])
     final_first(1)
     for c in range(CHUNKS):
-        sent_q(b_copy, c)
-    wait_z(r_copy, r_own, 1, 1)
+        wait_bytes(mid_out.at[c, pl.ds(0, 31)], bsend.at[c])
+    wait_bytes(recv_r.at[1, 1], rrecv.at[1, 1])
     final_second(1)
-    sent_z(r_copy, 0)
-    sent_z(r_copy, 1)
-    wait_z(r_copy, r_own, 2, 0)
+    wait_bytes(recv_r.at[0, :, pl.ds(0, 7)], rsend.at[0])
+    wait_bytes(recv_r.at[1, :, pl.ds(0, 7)], rsend.at[1])
+    wait_bytes(recv_r.at[2, 0], rrecv.at[2, 0])
     final_first(2)
-    wait_z(r_copy, r_own, 2, 1)
+    wait_bytes(recv_r.at[2, 1], rrecv.at[2, 1])
     final_second(2)
-    sent_z(r_copy, 2)
+    wait_bytes(recv_r.at[2, :, pl.ds(0, 7)], rsend.at[2])
 
 
 def solution(mesh):
@@ -375,14 +340,14 @@
                 pltpu.VMEM((2, 512, 512), BF16),
                 pltpu.SemaphoreType.DMA((CHUNKS,)),
                 pltpu.SemaphoreType.DMA((3,)),
-                pltpu.SemaphoreType.DMA((CHUNKS, 2, 8)),
-                pltpu.SemaphoreType.DMA((CHUNKS, 2, 8)),
-                pltpu.SemaphoreType.DMA((CHUNKS, 32)),
-                pltpu.SemaphoreType.DMA((CHUNKS, 32)),
-                pltpu.SemaphoreType.DMA((CHUNKS, 32)),
-                pltpu.SemaphoreType.DMA((CHUNKS, 32)),
-                pltpu.SemaphoreType.DMA((CHUNKS, 2, 8)),
-                pltpu.SemaphoreType.DMA((CHUNKS, 2, 8)),
+                pltpu.SemaphoreType.DMA((CHUNKS,)),
+                pltpu.SemaphoreType.DMA((CHUNKS, 2)),
+                pltpu.SemaphoreType.DMA((CHUNKS,)),
+                pltpu.SemaphoreType.DMA((CHUNKS,)),
+                pltpu.SemaphoreType.DMA((CHUNKS,)),
+                pltpu.SemaphoreType.DMA((CHUNKS, 2)),
+                pltpu.SemaphoreType.DMA((CHUNKS,)),
+                pltpu.SemaphoreType.DMA((CHUNKS, 2)),
             ],
             compiler_params=pltpu.CompilerParams(collective_id=0, has_side_effects=True, vmem_limit_bytes=40 * 2**20),
         )(*[pltpu.with_memory_space_constraint(a, pltpu.HBM) for a in (velocity, jnp.asarray(gdev), jnp.asarray(floc), jnp.asarray(twid))])

time: 157 us -> 152 us (0.968)
  Pallas kernels: 155 us -> 150 us
    pallas_call x1, Pallas kernels: 155 us -> 150 us  [step(): pl.pallas_call(kernel, out_shape=pltpu.VMEM(velocity.shape, F32), in_spec...]
where the time goes in v4:
time: 152 us
  Pallas kernels  150 us (99%)
  local copies, waits for them, and re-layouts  1.67 us (1%)
    pallas_call x1, Pallas kernels, step(): pl.pallas_call(kernel, out_shape=pltpu.VMEM(velocity.shape, F32), in_spec...  150 us

profile of v4, /device:TPU:8, one launch (start us, length us, event | category | flops | bytes accessed | tf_op | source)
XLA Modules:
  0.0 151.9 jit_solution(5276590501795532832)
XLA Ops:
  0.0 150.2 %shard_map.46 = f32[2,6,256,256]{3,2,1,0:T(8,128)S(1)} custom-call(f32[2,6,256,256]{3,2,1,0:T(8,128)} %x_hbm.1, bf16[2,512,512]{2,1,0:T(8,128)(2,1)} %constant.6.clone.gdev_hbm, f32[2,2,256,256]{3,2,1,0:T(8,128)} %constant.7.clone.floc_hbm, f32[2,16,2,8,256]{4,3,2,1,0:T(8,128)} %constant.8.clone.twid_hbm), custom_call_target="tpu_custom_call" | custom-call | tf_op jit(solution)/shard_map/pallas_call | solution.py:322
  150.2 1.7 %copy.6 = f32[2,6,256,256]{3,2,1,0:T(8,128)} copy(f32[2,6,256,256]{3,2,1,0:T(8,128)S(1)} %shard_map.46) | data formatting | bytes 6291456

commit v5 on v4

--- a/solution.py
+++ b/solution.py
@@ -63,9 +63,19 @@
     return jnp.dot(left, right, preferred_element_type=F32)
 
 
+def transformed(tiles, ytab, ztab):
+    flat = tiles.reshape(1024, 128)
+    rows = [jnp.concatenate([flat[pl.ds(p * 4 + s, 128, stride=8), :] for s in range(4)], axis=1) for p in range(2)]
+    xh, xl = split(jnp.concatenate(rows, axis=0))
+    v = mm(xh, ztab[0]) + mm(xl, ztab[0]) + mm(xh, ztab[1])
+    planes = [jnp.concatenate([v[p * 128 : p * 128 + 128, :256], v[p * 128 : p * 128 + 128, 256:]], axis=0) for p in range(2)]
+    vh, vl = split(jnp.concatenate(planes, axis=1))
+    return mm(ytab[0], vh) + mm(ytab[0], vl) + mm(ytab[1], vh)
+
+
 def kernel(
-    x_hbm, gdev_hbm, floc_hbm, twid_hbm, out,
-    xin, send_p, recv_p, mid_in, mid_out, recv_q, recv_r, part, gdev, floc, twid, ytab, ztab,
+    x_hbm, gdev_hbm, floc_hbm, twid_hbm, out, part, last, ytab, ztab,
+    xin, send_p, recv_p, mid_in, mid_out, recv_q, recv_r, gdev, floc, twid,
     in_sem, const_sem, psend, precv, qsend, qrecv, bsend, brecv, rsend, rrecv,
 ):
     gz, gy = lax.axis_index("gz"), lax.axis_index("gy")
@@ -91,8 +101,7 @@
         pltpu.make_async_copy(twid_hbm, twid, const_sem.at[1]),
         pltpu.make_async_copy(gdev_hbm, gdev, const_sem.at[2]),
     ]
-    for copy in loads + consts:
-        copy.start()
+    loads[0].start()
 
     barrier = pltpu.get_barrier_semaphore()
 
@@ -103,6 +112,9 @@
     @pl.loop(1, 32)
     def _(t):
         pl.semaphore_signal(barrier, inc=1, device_id=q_partner(t // 2, t % 2)[1], device_id_type=MESH)
+
+    for copy in loads[1:] + consts:
+        copy.start()
 
     def relayout(c, half):
         flat = send_p.at[c, half].reshape(1024, 128)
@@ -123,12 +135,15 @@
     def p_own(c, half):
         return pltpu.make_async_copy(send_p.at[c, half, z], recv_p.at[c, half, z], precv.at[c, half])
 
+    def returned(c, half):
+        return last if (c, half) == (CHUNKS - 1, 1) else recv_r.at[c, half]
+
     def r_copy(c, half, t):
         zt, device = z_partner(t)
-        return remote(recv_q.at[c, half, zt], recv_r.at[c, half, z], rsend.at[c], rrecv.at[c, half], device)
+        return remote(recv_q.at[c, half, zt], returned(c, half).at[z], rsend.at[c], rrecv.at[c, half], device)
 
     def r_own(c, half):
-        return pltpu.make_async_copy(recv_q.at[c, half, z], recv_r.at[c, half, z], rrecv.at[c, half])
+        return pltpu.make_async_copy(recv_q.at[c, half, z], returned(c, half).at[z], rrecv.at[c, half])
 
     def q_copy(c, t, dc):
         there, device = q_partner(t, dc)
@@ -219,20 +234,11 @@
         full = jnp.concatenate([jnp.concatenate([a, b], axis=1), jnp.concatenate([-b, a], axis=1)], axis=0)
         ztab[0], ztab[1] = split(full)
 
-    def transformed(c, half):
-        flat = recv_r.at[c, half].reshape(1024, 128)
-        rows = [jnp.concatenate([flat[pl.ds(p * 4 + s, 128, stride=8), :] for s in range(4)], axis=1) for p in range(2)]
-        xh, xl = split(jnp.concatenate(rows, axis=0))
-        v = mm(xh, ztab[0]) + mm(xl, ztab[0]) + mm(xh, ztab[1])
-        planes = [jnp.concatenate([v[p * 128 : p * 128 + 128, :256], v[p * 128 : p * 128 + 128, 256:]], axis=0) for p in range(2)]
-        vh, vl = split(jnp.concatenate(planes, axis=1))
-        return mm(ytab[half, 0], vh) + mm(ytab[half, 0], vl) + mm(ytab[half, 1], vh)
-
     def final_first(c):
-        part[...] = transformed(c, 0)
+        part[...] = transformed(recv_r.at[c, 0], ytab.at[0], ztab)
 
     def final_second(c):
-        u = part[...] + transformed(c, 1)
+        u = part[...] + transformed(recv_r.at[c, 1], ytab.at[1], ztab)
         for p in range(2):
             for r in range(2):
                 out[r, 2 * c + p] = u[r * 256 : r * 256 + 256, p * 256 : p * 256 + 256]
@@ -304,9 +310,24 @@
     wait_bytes(recv_r.at[1, :, pl.ds(0, 7)], rsend.at[1])
     wait_bytes(recv_r.at[2, 0], rrecv.at[2, 0])
     final_first(2)
-    wait_bytes(recv_r.at[2, 1], rrecv.at[2, 1])
-    final_second(2)
+    wait_bytes(last, rrecv.at[2, 1])
     wait_bytes(recv_r.at[2, :, pl.ds(0, 7)], rsend.at[2])
+
+
+def finish_kernel(done, part, last, ytab, ztab, o_hbm, rest, sems):
+    early = [pltpu.make_async_copy(done.at[r, a], o_hbm.at[r, a], sems.at[r, a]) for r in range(2) for a in range(4)]
+    for copy in early:
+        copy.start()
+    u = part[...] + transformed(last, ytab.at[1], ztab)
+    late = []
+    for p in range(2):
+        for r in range(2):
+            rest[r, p] = u[r * 256 : r * 256 + 256, p * 256 : p * 256 + 256]
+            copy = pltpu.make_async_copy(rest.at[r, p], o_hbm.at[r, 4 + p], sems.at[r, 4 + p])
+            copy.start()
+            late.append(copy)
+    for copy in early + late:
+        copy.wait()
 
 
 def solution(mesh):
@@ -319,11 +340,18 @@
         anywhere = pl.BlockSpec(memory_space=pl.ANY)
         halves = pltpu.VMEM((CHUNKS, 2, 8, 16, 8, 128), F32)
         middles = pltpu.VMEM((CHUNKS, 32, 8, 8, 128), F32)
-        return pl.pallas_call(
+        inside = pl.BlockSpec(memory_space=pltpu.VMEM)
+        held = pl.pallas_call(
             kernel,
-            out_shape=pltpu.VMEM(velocity.shape, F32),
+            out_shape=[
+                pltpu.VMEM((2, 4, 256, 256), F32),
+                pltpu.VMEM((512, 512), F32),
+                pltpu.VMEM((8, 16, 8, 128), F32),
+                pltpu.VMEM((2, 2, 512, 256), BF16),
+                pltpu.VMEM((2, 512, 512), BF16),
+            ],
             in_specs=[pl.BlockSpec(memory_space=pltpu.HBM)] * 4,
-            out_specs=pl.BlockSpec(memory_space=pltpu.VMEM),
+            out_specs=[inside] * 5,
             scratch_shapes=[
                 pltpu.VMEM((2, 6, 256, 256), F32),
                 halves,
@@ -332,12 +360,9 @@
                 middles,
                 halves,
                 halves,
-                pltpu.VMEM((512, 512), F32),
                 pltpu.VMEM((2, 512, 512), BF16),
                 pltpu.VMEM((2, 2, 256, 256), F32),
                 pltpu.VMEM((2, 16, 2, 8, 256), F32),
-                pltpu.VMEM((2, 2, 512, 256), BF16),
-                pltpu.VMEM((2, 512, 512), BF16),
                 pltpu.SemaphoreType.DMA((CHUNKS,)),
                 pltpu.SemaphoreType.DMA((3,)),
                 pltpu.SemaphoreType.DMA((CHUNKS,)),
@@ -351,6 +376,14 @@
             ],
             compiler_params=pltpu.CompilerParams(collective_id=0, has_side_effects=True, vmem_limit_bytes=40 * 2**20),
         )(*[pltpu.with_memory_space_constraint(a, pltpu.HBM) for a in (velocity, jnp.asarray(gdev), jnp.asarray(floc), jnp.asarray(twid))])
+        return pl.pallas_call(
+            finish_kernel,
+            out_shape=jax.ShapeDtypeStruct(velocity.shape, F32),
+            in_specs=[inside] * 5,
+            out_specs=anywhere,
+            scratch_shapes=[pltpu.VMEM((2, 2, 256, 256), F32), pltpu.SemaphoreType.DMA((2, 6))],
+            compiler_params=pltpu.CompilerParams(vmem_limit_bytes=16 * 2**20),
+        )(*[pltpu.with_memory_space_constraint(a, pltpu.VMEM) for a in held])
 
     return jax.shard_map(
         step, mesh=mesh, in_specs=(P(None, None, "gy", "gz"),), out_specs=P(None, None, "gy", "gz"), check_vma=False

time: 152 us -> 151 us (level)
  local copies, waits for them, and re-layouts: 1.67 us -> 0 us
    unnamed x1 -> x0, local copies, waits for them, and re-layouts: 1.67 us -> none
    pallas_call x1 -> x2, Pallas kernels: 150 us -> 151 us  [the longest x1 149 us: step(): pl.pallas_call(kernel, out_shape=[pltpu.VMEM((2, 4, 256, 256), F32), pltp...]
where the time goes in v5:
time: 151 us
  Pallas kernels  151 us (100%)
    pallas_call x1, Pallas kernels, step(): pl.pallas_call(kernel, out_shape=[pltpu.VMEM((2, 4, 256, 256), F32), pltp...  149 us

profile of v5, /device:TPU:8, one launch (start us, length us, event | category | flops | bytes accessed | tf_op | source)
XLA Modules:
  0.0 151.1 jit_solution(7506664087521879739)
XLA Ops:
  0.0 148.9 %shard_map.46 = (f32[2,4,256,256]{3,2,1,0:T(8,128)S(1)}, f32[512,512]{1,0:T(8,128)S(1)}, f32[8,16,8,128]{3,2,1,0:T(8,128)S(1)}, bf16[2,2,512,256]{3,2,1,0:T(8,128)(2,1)S(1)}, bf16[2,512,512]{2,1,0:T(8,128)(2,1)S(1)}) custom-call(f32[2,6,256,256]{3,2,1,0:T(8,128)} %x_hbm.1, bf16[2,512,512]{2,1,0:T(8,128)(2,1)} %constant.6.clone.gdev_hbm, ...), custom_call_target="tpu_custom_call" | custom-call | tf_op jit(solution)/shard_map/pallas_call | solution.py:344
  149.0 2.1 %shard_map.47 = f32[2,6,256,256]{3,2,1,0:T(8,128)} custom-call(f32[2,4,256,256]{3,2,1,0:T(8,128)S(1)} %get-tuple-element.10.done, f32[512,512]{1,0:T(8,128)S(1)} %get-tuple-element.11.part, f32[8,16,8,128]{3,2,1,0:T(8,128)S(1)} %get-tuple-element.12.last, bf16[2,2,512,256]{3,2,1,0:T(8,128)(2,1)S(1)} %get-tuple-element.13.ytab, ...), custom_call_target="tpu_custom_call" | custom-call | tf_op jit(solution)/shard_map/pallas_call | solution.py:379

commit v6 on v5

--- a/solution.py
+++ b/solution.py
@@ -63,13 +63,16 @@
     return jnp.dot(left, right, preferred_element_type=F32)
 
 
-def transformed(tiles, ytab, ztab):
+def z_transformed(tiles, ztab):
     flat = tiles.reshape(1024, 128)
     rows = [jnp.concatenate([flat[pl.ds(p * 4 + s, 128, stride=8), :] for s in range(4)], axis=1) for p in range(2)]
     xh, xl = split(jnp.concatenate(rows, axis=0))
     v = mm(xh, ztab[0]) + mm(xl, ztab[0]) + mm(xh, ztab[1])
-    planes = [jnp.concatenate([v[p * 128 : p * 128 + 128, :256], v[p * 128 : p * 128 + 128, 256:]], axis=0) for p in range(2)]
-    vh, vl = split(jnp.concatenate(planes, axis=1))
+    return [jnp.concatenate([v[p * 128 : p * 128 + 128, :256], v[p * 128 : p * 128 + 128, 256:]], axis=0) for p in range(2)]
+
+
+def y_sum(v, ytab):
+    vh, vl = split(v)
     return mm(ytab[0], vh) + mm(ytab[0], vl) + mm(ytab[1], vh)
 
 
@@ -235,10 +238,10 @@
         ztab[0], ztab[1] = split(full)
 
     def final_first(c):
-        part[...] = transformed(recv_r.at[c, 0], ytab.at[0], ztab)
+        part[...] = y_sum(jnp.concatenate(z_transformed(recv_r.at[c, 0], ztab), axis=1), ytab[0])
 
     def final_second(c):
-        u = part[...] + transformed(recv_r.at[c, 1], ytab.at[1], ztab)
+        u = part[...] + y_sum(jnp.concatenate(z_transformed(recv_r.at[c, 1], ztab), axis=1), ytab[1])
         for p in range(2):
             for r in range(2):
                 out[r, 2 * c + p] = u[r * 256 : r * 256 + 256, p * 256 : p * 256 + 256]
@@ -253,24 +256,25 @@
         loads[c].wait()
         relayout(c, 0)
         relayout(c, 1)
+        if c == 1:
+            start_z(p_copy, p_own, 1, 0)
+            start_z(p_copy, p_own, 1, 1)
     for copy in consts:
         copy.wait()
     tables()
     wait_bytes(recv_p.at[0, 0], precv.at[0, 0])
     start_q(0, 0)
-    start_z(p_copy, p_own, 1, 0)
+    start_z(p_copy, p_own, 2, 0)
     wait_bytes(recv_p.at[0, 1], precv.at[0, 1])
     start_q(0, 1)
-    start_z(p_copy, p_own, 1, 1)
+    start_z(p_copy, p_own, 2, 1)
     wait_bytes(mid_in.at[0], qrecv.at[0])
     middle(0)
     start_b(0)
     wait_bytes(recv_p.at[1, 0], precv.at[1, 0])
     start_q(1, 0)
-    start_z(p_copy, p_own, 2, 0)
     wait_bytes(recv_p.at[1, 1], precv.at[1, 1])
     start_q(1, 1)
-    start_z(p_copy, p_own, 2, 1)
     wait_bytes(recv_q.at[0, 0], brecv.at[0, 0])
     start_z(r_copy, r_own, 0, 0)
     wait_bytes(recv_q.at[0, 1], brecv.at[0, 1])
@@ -318,11 +322,11 @@
     early = [pltpu.make_async_copy(done.at[r, a], o_hbm.at[r, a], sems.at[r, a]) for r in range(2) for a in range(4)]
     for copy in early:
         copy.start()
-    u = part[...] + transformed(last, ytab.at[1], ztab)
     late = []
-    for p in range(2):
+    for p, v in enumerate(z_transformed(last, ztab)):
+        u = part[:, p * 256 : p * 256 + 256] + y_sum(v, ytab[1])
         for r in range(2):
-            rest[r, p] = u[r * 256 : r * 256 + 256, p * 256 : p * 256 + 256]
+            rest[r, p] = u[r * 256 : r * 256 + 256]
             copy = pltpu.make_async_copy(rest.at[r, p], o_hbm.at[r, 4 + p], sems.at[r, 4 + p])
             copy.start()
             late.append(copy)

time: 151 us -> 151 us (level)
  no operation moved by 1% of the time
where the time goes in v6:
time: 151 us
  Pallas kernels  151 us (100%)
    pallas_call x1, Pallas kernels, step(): pl.pallas_call(kernel, out_shape=[pltpu.VMEM((2, 4, 256, 256), F32), pltp...  149 us

profile of v6, /device:TPU:8, one launch (start us, length us, event | category | flops | bytes accessed | tf_op | source)
XLA Modules:
  0.0 151.1 jit_solution(7875187484560220020)
XLA Ops:
  0.0 148.9 %shard_map.46 = (f32[2,4,256,256]{3,2,1,0:T(8,128)S(1)}, f32[512,512]{1,0:T(8,128)S(1)}, f32[8,16,8,128]{3,2,1,0:T(8,128)S(1)}, bf16[2,2,512,256]{3,2,1,0:T(8,128)(2,1)S(1)}, bf16[2,512,512]{2,1,0:T(8,128)(2,1)S(1)}) custom-call(f32[2,6,256,256]{3,2,1,0:T(8,128)} %x_hbm.1, bf16[2,512,512]{2,1,0:T(8,128)(2,1)} %constant.6.clone.gdev_hbm, ...), custom_call_target="tpu_custom_call" | custom-call | tf_op jit(solution)/shard_map/pallas_call | solution.py:348
  149.0 2.1 %shard_map.47 = f32[2,6,256,256]{3,2,1,0:T(8,128)} custom-call(f32[2,4,256,256]{3,2,1,0:T(8,128)S(1)} %get-tuple-element.10.done, f32[512,512]{1,0:T(8,128)S(1)} %get-tuple-element.11.part, f32[8,16,8,128]{3,2,1,0:T(8,128)S(1)} %get-tuple-element.12.last, bf16[2,2,512,256]{3,2,1,0:T(8,128)(2,1)S(1)} %get-tuple-element.13.ytab, ...), custom_call_target="tpu_custom_call" | custom-call | tf_op jit(solution)/shard_map/pallas_call | solution.py:383
